TPU v7x, 32 devices: a whole 2x2x4 slice. The times are simulated.
32 devices in a mesh: groups: 2 (over y), dp: 8 (over z, x), tensor: 2 (over core).
Axes of the slice: x: 2, y: 2, z: 4, core: 2. Of those that a mesh axis runs over, the one named last changes fastest.
Arguments:
- hidden_acts: bfloat16 [16, 128, 14336], P(('groups', 'dp'), None, 'tensor'), parts along dimension 0, may hold values from -6 to 6
- out_grads: bfloat16 [16, 128, 4096], P(('groups', 'dp'), None, 'tensor'), parts along dimension 0, may hold values from -6 to 6
- token_ids: int32 [16, 128], P(('groups', 'dp')), parts along dimension 0, may hold values from 0 to 128255, as said below
- proj_in: bfloat16 [64, 14336], P(None, 'tensor'), may hold values from -0.046875 to 0.046875
- proj_out: bfloat16 [64, 4096], P(None, 'tensor'), may hold values from -0.09375 to 0.09375
- test_feats: bfloat16 [1024, 4096], P('dp'), may hold values from -0.3984375 to 0.3984375
- resample_counts: int32 [16, 256], P(('groups', 'dp')), parts along dimension 0, may hold values from 0 to 2, as said below
Outputs:
- scores: float32 [16, 1024], P(('groups', 'dp')), parts along dimension 0
- boot_sums: float32 [512, 1024], P(('groups', 'dp')), parts along dimension 0
There are 2 independent parts, one for each index of `groups`. A program takes and returns all parts, laid end to end along the dimension named above; an argument that names none is the same for every part. Nothing has to cross between parts.
Inputs may be any that keep to these rules, and one draw needn't show every extreme that they name: `token_ids`: each example is live from position 0 to its length and 0 after it; every example has at least 32 live tokens, which are never 0. `resample_counts`: for each resample b the counts over all examples sum to 8, and at least one example has count 2.
All inputs are finite; a program needn't handle non-finite values.
Results may differ from a plain program's by a relative error of at most 0.0029.
Values may be sent and summed in bfloat16 or wider, within the bound.
A program may use at most 64 MiB of HBM per device.

v0:
```python
import jax
import jax.numpy as jnp
from jax import lax
from jax.sharding import PartitionSpec as P


def shards(hidden_acts, out_grads, token_ids, proj_in, proj_out, test_feats, resample_counts):
    token_live = (token_ids != 0).astype(jnp.float32)
    live_count = jnp.sum(token_live, axis=1)
    in_part = jnp.einsum("rf,elf->erl", proj_in, hidden_acts, preferred_element_type=jnp.float32)
    out_part = jnp.einsum("rd,eld->erl", proj_out, out_grads, preferred_element_type=jnp.float32)
    in_feat, out_feat = lax.psum((in_part, out_part), "tensor")
    example_grad = (
        jnp.einsum(
            "eol,eil->eoi",
            out_feat * token_live[:, None, :],
            in_feat,
            precision=lax.Precision.HIGHEST,
        )
        / live_count[:, None, None]
    )
    train_feats = example_grad.reshape(example_grad.shape[0], -1).astype(jnp.bfloat16)
    score_cols = lax.dot_general(
        lax.all_gather(train_feats, "dp", axis=0, tiled=True),
        test_feats,
        (((1,), (1,)), ((), ())),
        preferred_element_type=jnp.float32,
    )
    all_counts = lax.all_gather(resample_counts, "dp", axis=0, tiled=True).astype(jnp.float32)
    boot_cols = lax.dot_general(
        all_counts,
        score_cols,
        (((0,), (0,)), ((), ())),
        precision=lax.Precision.HIGHEST,
        preferred_element_type=jnp.float32,
    )
    score_local, boot_sums = (
        lax.all_to_all(score_cols, "dp", split_axis=0, concat_axis=1, tiled=True),
        lax.all_to_all(boot_cols, "dp", split_axis=0, concat_axis=1, tiled=True),
    )
    return (score_local, boot_sums)


def solution(mesh):
    placed = (
        P(("groups", "dp"), None, "tensor"),
        P(("groups", "dp"), None, "tensor"),
        P(("groups", "dp"), None),
        P(None, "tensor"),
        P(None, "tensor"),
        P("dp", None),
        P(("groups", "dp"), None),
    )
    return jax.shard_map(
        shards,
        mesh=mesh,
        in_specs=placed,
        out_specs=(P(("groups", "dp"), None), P(("groups", "dp"), None)),
        check_vma=False,
    )
```

profile of v0, /device:TPU:0, one launch (start us, length us, event | category | flops | bytes accessed | tf_op | source)
XLA Modules:
  0.0 96.9 jit_solution(11531436528812818203)
XLA Ops:
  7.2 0.0 copy-start
  7.2 0.0 copy-start.2
  7.2 0.0 copy-start.5
  7.2 0.0 copy-start.4
  7.2 0.0 copy-start.1
  7.2 0.0 all-reduce.3.cloned.1.call-start
  7.3 1.4 %copy-done = bf16[1,128,7168]{2,1,0:T(8,128)(2,1)S(1)} copy-done((bf16[1,128,7168]{2,1,0:T(8,128)(2,1)S(1)}, bf16[1,128,7168]{2,1,0:T(8,128)(2,1)}, u32[]{:S(2)}) %copy-start) | copy-done | bytes 1835032
  8.7 0.0 copy-start.3
  8.7 2.6 %fusion.2 = f32[64,128]{1,0:T(8,128)} fusion(bf16[64,7168]{1,0:T(8,128)(2,1)} %param.10, bf16[1,128,7168]{2,1,0:T(8,128)(2,1)S(1)} %copy-done), kind=kOutput, calls=%fused_computation.3 | convolution fusion | flops 117440512 | bytes 2785280 | tf_op jit(solution)/shard_map/rf,elf->erl/dot_general | solution.py:10
  11.3 0.0 copy-done.2
  11.3 0.0 copy-done.3
  11.3 0.9 convolution_bitcast_fusion.1
  12.2 0.0 all-reduce.3.cloned.1.call-update
  12.2 0.0 copy-done.5
  12.2 0.0 copy-done.4
  12.2 22.2 %all-gather.1 = s32[8,1,256]{2,1,0:T(1,128)S(1)} all-gather(s32[1,1,256]{2,1,0:T(1,128)S(1)} %bitcast.49), channel_id=1, replica_groups=mesh['groups'=2,'dp'=8,'tensor'=2] {'dp'}, dimensions={0}, use_global_device_ids=true | all-gather | bytes 9216 | tf_op jit(solution)/shard_map/all_gather | solution.py:29
  34.5 0.6 fusion.15
  35.1 0.0 all-reduce.3.cloned.1.call-done
  35.1 1.6 %fusion.5 = bf16[64,64]{1,0:T(8,128)(2,1)S(1)} fusion(f32[64,128]{1,0:T(8,128)} %get-tuple-element.2, f32[1,64,128]{2,1,0:T(8,128)} %get-tuple-element.3, f32[]{:T(128)} %fusion.15, f32[128]{0:T(128)S(1)} %fusion.16), kind=kOutput, calls=%fused_computation.6 | convolution fusion | flops 6307840 | bytes 74244 | tf_op jit(solution)/shard_map/eol,eil->eoi/dot_general | solution.py:14
  36.7 0.1 reshape.56
  36.8 30.6 %all-gather = bf16[8,1,4096]{2,1,0:T(2,128)(2,1)S(1)} all-gather(bf16[1,1,4096]{2,1,0:T(2,128)(2,1)S(1)} %reshape.56), channel_id=1, replica_groups=mesh['groups'=2,'dp'=8,'tensor'=2] {'dp'}, dimensions={0}, use_global_device_ids=true | all-gather | bytes 73728 | tf_op jit(solution)/shard_map/all_gather | solution.py:24
  67.4 0.0 copy-done.1
  67.4 1.0 %fusion.7 = f32[8,128]{1,0:T(8,128)} fusion(bf16[128,4096]{1,0:T(8,128)(2,1)S(1)} %copy-done.1, bf16[8,1,4096]{2,1,0:T(2,128)(2,1)S(1)} %all-gather), kind=kOutput, calls=%fused_computation.9 | convolution fusion | flops 8388608 | bytes 1118208 | tf_op jit(solution)/shard_map/dot_general | solution.py:23
  68.4 3.4 %all-to-all-start = ((f32[8,1,128]{2,1,0:T(1,128)}), f32[8,1,128]{2,1,0:T(1,128)S(1)}, u32[]{:S(2)}, u32[]{:S(2)}) async-start(f32[8,1,128]{2,1,0:T(1,128)} %bitcast.10), calls=%async_computation | async-start | bytes 8192 | tf_op jit(solution)/shard_map/all_to_all | solution.py:38
  71.8 1.0 %convolution_bitcast_fusion = f32[256,128]{0,1:T(8,128)S(1)} fusion(f32[8,128]{1,0:T(8,128)} %fusion.7, f32[8,1,256]{2,1,0:T(1,128)S(1)} %convert_element_type.24), kind=kOutput, calls=%fused_computation.2 | convolution fusion | flops 3145728 | bytes 143360 | tf_op jit(solution)/shard_map/dot_general | solution.py:30
  72.8 0.8 copy.16
  73.6 4.6 %all-to-all-done = f32[8,1,128]{2,1,0:T(1,128)S(1)} async-done(((f32[8,1,128]{2,1,0:T(1,128)}), f32[8,1,128]{2,1,0:T(1,128)S(1)}, u32[]{:S(2)}, u32[]{:S(2)}) %all-to-all-start) | async-done | bytes 4128 | tf_op jit(solution)/shard_map/all_to_all | solution.py:38
  78.2 3.4 %all-to-all-start.1 = ((f32[8,32,128]{2,1,0:T(8,128)}), f32[8,32,128]{2,1,0:T(8,128)S(1)}, u32[]{:S(2)}, u32[]{:S(2)}) async-start(f32[8,32,128]{2,1,0:T(8,128)} %bitcast.14), calls=%async_computation.1 | async-start | bytes 262144 | tf_op jit(solution)/shard_map/all_to_all | solution.py:39
  81.5 7.3 %all-to-all-done.1 = f32[8,32,128]{2,1,0:T(8,128)S(1)} async-done(((f32[8,32,128]{2,1,0:T(8,128)}), f32[8,32,128]{2,1,0:T(8,128)S(1)}, u32[]{:S(2)}, u32[]{:S(2)}) %all-to-all-start.1) | async-done | bytes 131104 | tf_op jit(solution)/shard_map/all_to_all | solution.py:39
  88.8 0.7 copy_bitcast_fusion
  89.5 0.6 copy.33
  (2 shorter events, 0.0 us)
Async XLA Ops:
  7.2 1.5 %copy-start = (bf16[1,128,7168]{2,1,0:T(8,128)(2,1)S(1)}, bf16[1,128,7168]{2,1,0:T(8,128)(2,1)}, u32[]{:S(2)}) copy-start(bf16[1,128,7168]{2,1,0:T(8,128)(2,1)} %param.7) | copy-start | bytes 5505028
  7.2 4.1 %copy-start.2 = (bf16[1,128,2048]{2,1,0:T(8,128)(2,1)S(1)}, bf16[1,128,2048]{2,1,0:T(8,128)(2,1)}, u32[]{:S(2)}) copy-start(bf16[1,128,2048]{2,1,0:T(8,128)(2,1)} %param.8) | copy-start | bytes 1572868
  7.2 5.0 %copy-start.5 = (s32[1,128]{1,0:T(1,128)S(1)}, s32[1,128]{1,0:T(1,128)}, u32[]{:S(2)}) copy-start(s32[1,128]{1,0:T(1,128)} %param.9) | copy-start | bytes 1540
  7.2 5.0 %copy-start.4 = (s32[1,256]{1,0:T(1,128)S(1)}, s32[1,256]{1,0:T(1,128)}, u32[]{:S(2)}) copy-start(s32[1,256]{1,0:T(1,128)} %param.13) | copy-start | bytes 3076
  7.2 60.2 %copy-start.1 = (bf16[128,4096]{1,0:T(8,128)(2,1)S(1)}, bf16[128,4096]{1,0:T(8,128)(2,1)}, u32[]{:S(2)}) copy-start(bf16[128,4096]{1,0:T(8,128)(2,1)} %param.12) | copy-start | bytes 3145732
  7.2 27.9 %all-reduce.3.cloned.1.call-start = ((), (), s32[]{:S(2)}) async-start(), calls=%async_computation.2 | async-start | bytes 131072 | tf_op jit(solution)/shard_map/psum | solution.py:12
  8.7 2.6 %copy-start.3 = (bf16[64,2048]{1,0:T(8,128)(2,1)S(1)}, bf16[64,2048]{1,0:T(8,128)(2,1)}, u32[]{:S(2)}) copy-start(bf16[64,2048]{1,0:T(8,128)(2,1)} %param.11) | copy-start | bytes 786436
  68.4 9.8 %all-to-all-start = ((f32[8,1,128]{2,1,0:T(1,128)}), f32[8,1,128]{2,1,0:T(1,128)S(1)}, u32[]{:S(2)}, u32[]{:S(2)}) async-start(f32[8,1,128]{2,1,0:T(1,128)} %bitcast.10), calls=%async_computation | async-start | bytes 8192 | tf_op jit(solution)/shard_map/all_to_all | solution.py:38
  78.2 10.7 %all-to-all-start.1 = ((f32[8,32,128]{2,1,0:T(8,128)}), f32[8,32,128]{2,1,0:T(8,128)S(1)}, u32[]{:S(2)}, u32[]{:S(2)}) async-start(f32[8,32,128]{2,1,0:T(8,128)} %bitcast.14), calls=%async_computation.1 | async-start | bytes 262144 | tf_op jit(solution)/shard_map/all_to_all | solution.py:39
Sparse Core Ops, SparseCore 0:
  12.3 20.4 all-reduce.2
where the time goes:
time: 97.3 us; the launch traced here: 96.9 us
  blocking collectives  52.9 us (54%)
  between operations  14.1 us (14%)
  waiting for transfers between devices  11.9 us (12%)
  matrix products  7.12 us (7%)
  starting transfers between devices  6.81 us (7%)
  local copies, waits for them, and re-layouts  3.53 us (4%)
    all_gather x1, blocking collectives, shards(): lax.all_gather(train_feats, 'dp', axis=0, tiled=True)  30.6 us
    all_gather x1, blocking collectives, shards(): lax.all_gather(resample_counts, 'dp', axis=0, tiled=True)  22.2 us
    all_to_all x1, waiting for transfers between devices, shards(): lax.all_to_all(boot_cols, 'dp', split_axis=0, concat_axis=1, tiled=True)  7.28 us
    all_to_all x1, waiting for transfers between devices, shards(): lax.all_to_all(score_cols, 'dp', split_axis=0, concat_axis=1, tiled=True)  4.58 us
    all_to_all x1, starting transfers between devices, shards(): lax.all_to_all(score_cols, 'dp', split_axis=0, concat_axis=1, tiled=True)  3.4 us
    all_to_all x1, starting transfers between devices, shards(): lax.all_to_all(boot_cols, 'dp', split_axis=0, concat_axis=1, tiled=True)  3.37 us
    dot_general x1, matrix products, shards(): jnp.einsum('rf,elf->erl', proj_in, hidden_acts, preferred_element_type=jn...  2.59 us
    unnamed x14, local copies, waits for them, and re-layouts  2.11 us
  transfers between devices with their start and end apart: 3, of which 2 were waited for; matrix products, arithmetic and copies ran while one was open for 2% of the time, Pallas kernels for 0%

commit v1 on v0

--- a/solution.py
+++ b/solution.py
@@ -1,7 +1,15 @@
+import functools
+
 import jax
 import jax.numpy as jnp
 from jax import lax
+from jax.experimental import pallas as pl
+from jax.experimental.pallas import tpu as pltpu
 from jax.sharding import PartitionSpec as P
+
+MESH = pl.DeviceIdType.MESH
+F32 = jnp.float32
+NT = (((1,), (1,)), ((), ()))
 
 
 def shards(hidden_acts, out_grads, token_ids, proj_in, proj_out, test_feats, resample_counts):
@@ -41,7 +49,192 @@
     return (score_local, boot_sums)
 
 
+def kernel(
+    n, chunks,
+    hid_hbm, grad_hbm, tok_hbm, pin_hbm, pout_hbm, test_hbm, cnt_hbm,
+    score_ref, boot_ref,
+    hid, grad, tok, pin, pout, test, cnt, part, other, feats, wide, every,
+    load_sem, chunk_sem, pair_sem, cnt_send, cnt_recv, feat_send, feat_recv, sc_send, sc_recv,
+):
+    me = lax.axis_index("dp")
+    core = lax.axis_index("tensor")
+    rank = pout.shape[0]
+    half = rank // 2
+    tests = test.shape[0]
+    boots = boot_ref.shape[0]
+    peers = [lax.rem(me + k, n) for k in range(1, n)]
+    froms = [lax.rem(me + n - k, n) for k in range(1, n)]
+
+    barrier = pltpu.get_barrier_semaphore()
+    pl.semaphore_signal(barrier, inc=1, device_id={"tensor": 1 - core}, device_id_type=MESH)
+    for peer in peers:
+        pl.semaphore_signal(barrier, inc=1, device_id={"dp": peer}, device_id_type=MESH)
+
+    def load(src, dst, sem):
+        copy = pltpu.make_async_copy(src, dst, sem)
+        copy.start()
+        return copy
+
+    load_pout = load(pout_hbm, pout, load_sem.at[0])
+    load_grad = load(grad_hbm.at[0], grad, load_sem.at[1])
+    width = hid.shape[1] // chunks
+    loads = []
+    for c in range(chunks):
+        cols = pl.ds(c * width, width)
+        loads.append((
+            load(pin_hbm.at[:, cols], pin.at[:, cols], chunk_sem.at[0, c]),
+            load(hid_hbm.at[0, :, cols], hid.at[:, cols], chunk_sem.at[1, c]),
+        ))
+    mine = pl.ds(me, 1)
+    load_cnt = load(cnt_hbm, cnt.at[mine, :], load_sem.at[2])
+    load_tok = load(tok_hbm, tok, load_sem.at[3])
+    load_test = load(test_hbm, test, load_sem.at[4])
+
+    load_pout.wait()
+    load_grad.wait()
+    part[0:rank, :] = lax.dot_general(pout[...], grad[...], NT, preferred_element_type=F32)
+    total = None
+    for c in range(chunks):
+        for copy in loads[c]:
+            copy.wait()
+        cols = slice(c * width, (c + 1) * width)
+        term = lax.dot_general(pin[:, cols], hid[:, cols], NT, preferred_element_type=F32)
+        total = term if total is None else total + term
+    part[rank:, :] = total
+
+    pl.semaphore_wait(barrier, n)
+    pair = pltpu.make_async_remote_copy(
+        src_ref=part, dst_ref=other, send_sem=pair_sem.at[0], recv_sem=pair_sem.at[1],
+        device_id={"tensor": 1 - core}, device_id_type=MESH,
+    )
+    pair.start()
+
+    load_cnt.wait()
+    sends = []
+
+    def to_all(ref, send_sem, recv_sem):
+        for k, peer in enumerate(peers):
+            copy = pltpu.make_async_remote_copy(
+                src_ref=ref, dst_ref=ref, send_sem=send_sem.at[k], recv_sem=recv_sem.at[k],
+                device_id={"dp": peer}, device_id_type=MESH,
+            )
+            copy.start()
+            sends.append(copy)
+
+    def arrived(ref, k, send_sem, recv_sem):
+        pltpu.make_async_remote_copy(
+            src_ref=ref, dst_ref=ref, send_sem=send_sem.at[k], recv_sem=recv_sem.at[k],
+            device_id={"dp": peers[k]}, device_id_type=MESH,
+        ).wait_recv()
+
+    to_all(cnt.at[mine, :], cnt_send, cnt_recv)
+    load_tok.wait()
+    live = (tok[...] != 0).astype(F32)
+    live_count = jnp.sum(live, axis=1, keepdims=True)
+
+    pair.wait_recv()
+    even, odd = pl.ds(0, half, stride=2), pl.ds(1, half, stride=2)
+    out_even = (part[even, :] + other[even, :]) * live
+    out_odd = (part[odd, :] + other[odd, :]) * live
+    in_feat = part[rank:, :] + other[rank:, :]
+    blank = jnp.zeros_like(in_feat)
+    grads = lax.dot_general(
+        jnp.concatenate([out_even, out_odd], axis=1),
+        jnp.concatenate(
+            [jnp.concatenate([in_feat, blank], axis=1), jnp.concatenate([blank, in_feat], axis=1)], axis=0
+        ),
+        NT,
+        precision=lax.Precision.HIGHEST,
+        preferred_element_type=F32,
+    )
+    feats[me] = (grads / live_count).astype(jnp.bfloat16)
+    to_all(feats.at[me], feat_send, feat_recv)
+
+    for k in range(n - 1):
+        arrived(cnt.at[pl.ds(froms[k], 1), :], k, cnt_send, cnt_recv)
+    row = lax.broadcasted_iota(jnp.int32, (boots, cnt.shape[1]), 0)
+    col = lax.broadcasted_iota(jnp.int32, (boots, cnt.shape[1]), 1)
+    pick = (col == row + me * boots).astype(F32)
+    my_counts = lax.dot_general(
+        pick, cnt[...].astype(F32), NT, precision=lax.Precision.HIGHEST, preferred_element_type=F32
+    )
+
+    def widen(source):
+        rows = pl.ds(pl.multiple_of(source * half, half), half)
+        wide[rows, :] = feats[source].astype(F32)
+
+    widen(me)
+    load_test.wait()
+    for k in range(n - 1):
+        arrived(feats.at[froms[k]], k, feat_send, feat_recv)
+        widen(froms[k])
+    flat = jnp.concatenate([wide[pl.ds(r, n, stride=half), :] for r in range(half)], axis=1)
+    scores = lax.dot_general(flat.astype(jnp.bfloat16), test[...], NT, preferred_element_type=F32)
+
+    def place(source):
+        return pl.ds(pl.multiple_of(source * tests, tests), tests)
+
+    every[:, place(me)] = scores
+    to_all(every.at[:, place(me)], sc_send, sc_recv)
+    for k in range(n - 1):
+        arrived(every.at[:, place(froms[k])], k, sc_send, sc_recv)
+    score_ref[...] = every[mine, :]
+    boot_ref[...] = jnp.dot(my_counts, every[...], precision=lax.Precision.HIGHEST, preferred_element_type=F32)
+
+    pair.wait_send()
+    for copy in sends:
+        copy.wait_send()
+
+
+def fused(n, hidden_acts, out_grads, token_ids, proj_in, proj_out, test_feats, resample_counts):
+    _, tokens, units = hidden_acts.shape
+    rank, model = proj_out.shape
+    tests = test_feats.shape[0]
+    boots = resample_counts.shape[1]
+    chunks = 4 if units % (4 * 128) == 0 else 1
+    dma = pltpu.SemaphoreType.DMA
+    any_spec = pl.BlockSpec(memory_space=pl.ANY)
+    vmem = pl.BlockSpec(memory_space=pltpu.VMEM)
+    return pl.pallas_call(
+        functools.partial(kernel, n, chunks),
+        out_shape=(
+            jax.ShapeDtypeStruct((1, n * tests), F32),
+            jax.ShapeDtypeStruct((boots // n, n * tests), F32),
+        ),
+        in_specs=[any_spec] * 7,
+        out_specs=(vmem, vmem),
+        scratch_shapes=[
+            pltpu.VMEM((tokens, units), jnp.bfloat16),
+            pltpu.VMEM((tokens, model), jnp.bfloat16),
+            pltpu.VMEM((1, tokens), jnp.int32),
+            pltpu.VMEM((rank, units), jnp.bfloat16),
+            pltpu.VMEM((rank, model), jnp.bfloat16),
+            pltpu.VMEM(test_feats.shape, jnp.bfloat16),
+            pltpu.VMEM((n, boots), jnp.int32),
+            pltpu.VMEM((2 * rank, tokens), F32),
+            pltpu.VMEM((2 * rank, tokens), F32),
+            pltpu.VMEM((n, rank // 2, 2 * rank), jnp.bfloat16),
+            pltpu.VMEM((n * rank // 2, 2 * rank), F32),
+            pltpu.VMEM((n, n * tests), F32),
+            dma((5,)),
+            dma((2, chunks)),
+            dma((2,)),
+        ] + [dma((n - 1,))] * 6,
+        compiler_params=pltpu.CompilerParams(
+            collective_id=0, has_side_effects=True, vmem_limit_bytes=32 * 1024 * 1024
+        ),
+        cost_estimate=pl.CostEstimate(flops=300_000_000, bytes_accessed=5_000_000, transcendentals=0),
+    )(hidden_acts, out_grads, token_ids, proj_in, proj_out, test_feats, resample_counts)
+
+
 def solution(mesh):
+    n = mesh.shape["dp"]
+
+    def body(*args):
+        if args[0].shape[0] == 1 and args[5].shape[0] % 128 == 0:
+            return fused(n, *args)
+        return shards(*args)
+
     placed = (
         P(("groups", "dp"), None, "tensor"),
         P(("groups", "dp"), None, "tensor"),
@@ -52,7 +245,7 @@
         P(("groups", "dp"), None),
     )
     return jax.shard_map(
-        shards,
+        body,
         mesh=mesh,
         in_specs=placed,
         out_specs=(P(("groups", "dp"), None), P(("groups", "dp"), None)),

time: 97.3 us -> 26.2 us (0.27)
  blocking collectives: 52.9 us -> 0 us
  Pallas kernels: 0 us -> 16.7 us
  between operations: 14.1 us -> 0.66 us
  waiting for transfers between devices: 11.9 us -> 0 us
  matrix products: 7.12 us -> 0 us
  starting transfers between devices: 6.81 us -> 0 us
  local copies, waits for them, and re-layouts: 3.53 us -> 8.47 us
    all_gather x2 -> x0, blocking collectives: 52.9 us -> none  [the longest x1 30.6 us: shards(): lax.all_gather(train_feats, 'dp', axis=0, tiled=True)]
    pallas_call x0 -> x1, Pallas kernels: none -> 16.7 us  [fused(): pl.pallas_call(functools.partial(kernel, n, chunks), out_shape=(jax.Shape...]
    all_to_all x2 -> x0, waiting for transfers between devices: 11.9 us -> none  [the longest x1 7.28 us: shards(): lax.all_to_all(boot_cols, 'dp', split_axis=0, concat_axis=1, tiled=True)]
    dot_general x5 -> x0, matrix products: 7.12 us -> none  [the longest x1 2.59 us: shards(): jnp.einsum('rf,elf->erl', proj_in, hidden_acts, preferred_element_type=jn...]
    all_to_all x2 -> x0, starting transfers between devices: 6.77 us -> none  [the longest x1 3.4 us: shards(): lax.all_to_all(score_cols, 'dp', split_axis=0, concat_axis=1, tiled=True)]
    unnamed x14 -> x16, local copies, waits for them, and re-layouts: 2.11 us -> 8.47 us
  transfers between devices with their start and end apart: 3 -> 0, of which waited for: 2 -> 0; matrix products, arithmetic and copies ran while one was open for 2% -> 0% of each run, Pallas kernels for 0% -> 0%
where the time goes in v1:
time: 26.2 us; the launch traced here: 25.8 us
  Pallas kernels  16.7 us (64%)
  local copies, waits for them, and re-layouts  8.47 us (32%)
  between operations  0.66 us (3%)
    pallas_call x1, Pallas kernels, fused(): pl.pallas_call(functools.partial(kernel, n, chunks), out_shape=(jax.Shape...  16.7 us
    unnamed x16, local copies, waits for them, and re-layouts  8.47 us

profile of v1, /device:TPU:0, one launch (start us, length us, event | category | flops | bytes accessed | tf_op | source)
XLA Modules:
  0.0 25.8 jit_solution(17132131957957459424)
XLA Ops:
  0.6 0.0 copy-start
  0.6 1.5 %copy-done = bf16[1,128,7168]{2,1,0:T(8,128)(2,1)S(1)} copy-done((bf16[1,128,7168]{2,1,0:T(8,128)(2,1)S(1)}, bf16[1,128,7168]{2,1,0:T(8,128)(2,1)}, u32[]{:S(2)}) %copy-start) | copy-done | bytes 1835032
  2.1 0.0 copy-start.1
  2.1 1.2 %copy-done.1 = bf16[128,4096]{1,0:T(8,128)(2,1)S(1)} copy-done((bf16[128,4096]{1,0:T(8,128)(2,1)S(1)}, bf16[128,4096]{1,0:T(8,128)(2,1)}, u32[]{:S(2)}) %copy-start.1) | copy-done | bytes 1048600
  3.4 0.0 copy-start.2
  3.4 1.2 %copy-done.2 = bf16[64,7168]{1,0:T(8,128)(2,1)S(1)} copy-done((bf16[64,7168]{1,0:T(8,128)(2,1)S(1)}, bf16[64,7168]{1,0:T(8,128)(2,1)}, u32[]{:S(2)}) %copy-start.2) | copy-done | bytes 917528
  4.5 0.0 copy-start.3
  4.5 1.0 %copy-done.3 = bf16[1,128,2048]{2,1,0:T(8,128)(2,1)S(1)} copy-done((bf16[1,128,2048]{2,1,0:T(8,128)(2,1)S(1)}, bf16[1,128,2048]{2,1,0:T(8,128)(2,1)}, u32[]{:S(2)}) %copy-start.3) | copy-done | bytes 524312
  5.6 0.0 copy-start.4
  5.6 0.9 %copy-done.4 = bf16[64,2048]{1,0:T(8,128)(2,1)S(1)} copy-done((bf16[64,2048]{1,0:T(8,128)(2,1)S(1)}, bf16[64,2048]{1,0:T(8,128)(2,1)}, u32[]{:S(2)}) %copy-start.4) | copy-done | bytes 262168
  6.5 0.0 copy-start.5
  6.5 0.7 %copy-done.5 = s32[1,256]{1,0:T(1,128)S(1)} copy-done((s32[1,256]{1,0:T(1,128)S(1)}, s32[1,256]{1,0:T(1,128)}, u32[]{:S(2)}) %copy-start.5) | copy-done | bytes 1048
  7.2 0.0 copy-start.6
  7.2 0.7 %copy-done.6 = s32[1,128]{1,0:T(1,128)S(1)} copy-done((s32[1,128]{1,0:T(1,128)S(1)}, s32[1,128]{1,0:T(1,128)}, u32[]{:S(2)}) %copy-start.6) | copy-done | bytes 536
  7.9 16.7 %shard_map.86 = (f32[1,1024]{1,0:T(1,128)S(1)}, f32[32,1024]{1,0:T(8,128)S(1)}) custom-call(bf16[1,128,7168]{2,1,0:T(8,128)(2,1)S(1)} %copy-done, bf16[1,128,2048]{2,1,0:T(8,128)(2,1)S(1)} %copy-done.3, s32[1,128]{1,0:T(1,128)S(1)} %copy-done.6, bf16[64,7168]{1,0:T(8,128)(2,1)S(1)} %copy-done.2, bf16[64,2048]{1,0:T(8,128)(2,1)S(1)} %copy-done.4, ...), custom_call_target="tpu_custom_call" | custom-call | flops 300000000 | bytes 5000000 | tf_op jit(solution)/shard_map/pallas_call | solution.py:198
  24.6 0.6 %copy.11 = f32[1,1024]{1,0:T(1,128)} copy(f32[1,1024]{1,0:T(1,128)S(1)} %get-tuple-element.4) | data formatting | bytes 8192
  25.2 0.7 %copy.12 = f32[32,1024]{1,0:T(8,128)} copy(f32[32,1024]{1,0:T(8,128)S(1)} %get-tuple-element.5) | data formatting | bytes 262144
Async XLA Ops:
  0.6 1.5 %copy-start = (bf16[1,128,7168]{2,1,0:T(8,128)(2,1)S(1)}, bf16[1,128,7168]{2,1,0:T(8,128)(2,1)}, u32[]{:S(2)}) copy-start(bf16[1,128,7168]{2,1,0:T(8,128)(2,1)} %hid_hbm.1) | copy-start | bytes 5505028
  2.1 1.2 %copy-start.1 = (bf16[128,4096]{1,0:T(8,128)(2,1)S(1)}, bf16[128,4096]{1,0:T(8,128)(2,1)}, u32[]{:S(2)}) copy-start(bf16[128,4096]{1,0:T(8,128)(2,1)} %test_hbm.1) | copy-start | bytes 3145732
  3.4 1.2 %copy-start.2 = (bf16[64,7168]{1,0:T(8,128)(2,1)S(1)}, bf16[64,7168]{1,0:T(8,128)(2,1)}, u32[]{:S(2)}) copy-start(bf16[64,7168]{1,0:T(8,128)(2,1)} %pin_hbm.1) | copy-start | bytes 2752516
  4.5 1.0 %copy-start.3 = (bf16[1,128,2048]{2,1,0:T(8,128)(2,1)S(1)}, bf16[1,128,2048]{2,1,0:T(8,128)(2,1)}, u32[]{:S(2)}) copy-start(bf16[1,128,2048]{2,1,0:T(8,128)(2,1)} %grad_hbm.1) | copy-start | bytes 1572868
  5.6 0.9 %copy-start.4 = (bf16[64,2048]{1,0:T(8,128)(2,1)S(1)}, bf16[64,2048]{1,0:T(8,128)(2,1)}, u32[]{:S(2)}) copy-start(bf16[64,2048]{1,0:T(8,128)(2,1)} %pout_hbm.1) | copy-start | bytes 786436
  6.5 0.7 %copy-start.5 = (s32[1,256]{1,0:T(1,128)S(1)}, s32[1,256]{1,0:T(1,128)}, u32[]{:S(2)}) copy-start(s32[1,256]{1,0:T(1,128)} %cnt_hbm.1) | copy-start | bytes 3076
  7.2 0.7 %copy-start.6 = (s32[1,128]{1,0:T(1,128)S(1)}, s32[1,128]{1,0:T(1,128)}, u32[]{:S(2)}) copy-start(s32[1,128]{1,0:T(1,128)} %tok_hbm.1) | copy-start | bytes 1540

commit v2 on v1

--- a/solution.py
+++ b/solution.py
@@ -193,7 +193,7 @@
     boots = resample_counts.shape[1]
     chunks = 4 if units % (4 * 128) == 0 else 1
     dma = pltpu.SemaphoreType.DMA
-    any_spec = pl.BlockSpec(memory_space=pl.ANY)
+    in_hbm = pl.BlockSpec(memory_space=pl.ANY)
     vmem = pl.BlockSpec(memory_space=pltpu.VMEM)
     return pl.pallas_call(
         functools.partial(kernel, n, chunks),
@@ -201,7 +201,7 @@
             jax.ShapeDtypeStruct((1, n * tests), F32),
             jax.ShapeDtypeStruct((boots // n, n * tests), F32),
         ),
-        in_specs=[any_spec] * 7,
+        in_specs=[in_hbm] * 7,
         out_specs=(vmem, vmem),
         scratch_shapes=[
             pltpu.VMEM((tokens, units), jnp.bfloat16),
@@ -221,7 +221,7 @@
             dma((2,)),
         ] + [dma((n - 1,))] * 6,
         compiler_params=pltpu.CompilerParams(
-            collective_id=0, has_side_effects=True, vmem_limit_bytes=32 * 1024 * 1024
+            collective_id=0, has_side_effects=True, vmem_limit_bytes=60 * 1024 * 1024
         ),
         cost_estimate=pl.CostEstimate(flops=300_000_000, bytes_accessed=5_000_000, transcendentals=0),
     )(hidden_acts, out_grads, token_ids, proj_in, proj_out, test_feats, resample_counts)

time: 26.2 us -> 21.1 us (0.81)
  local copies, waits for them, and re-layouts: 8.47 us -> 2.85 us
  Pallas kernels: 16.7 us -> 17.4 us
    unnamed x16 -> x2, local copies, waits for them, and re-layouts: 8.47 us -> 2.85 us
    pallas_call x1, Pallas kernels: 16.7 us -> 17.4 us  [fused(): pl.pallas_call(functools.partial(kernel, n, chunks), out_shape=(jax.Shape...]
where the time goes in v2:
time: 21.1 us; the launch traced here: 20.9 us
  Pallas kernels  17.4 us (82%)
  local copies, waits for them, and re-layouts  2.85 us (14%)
  between operations  0.64 us (3%)
    pallas_call x1, Pallas kernels, fused(): pl.pallas_call(functools.partial(kernel, n, chunks), out_shape=(jax.Shape...  17.4 us
    unnamed x2, local copies, waits for them, and re-layouts  2.85 us

profile of v2, /device:TPU:0, one launch (start us, length us, event | category | flops | bytes accessed | tf_op | source)
XLA Modules:
  0.0 20.9 jit_solution(2397140896623645184)
XLA Ops:
  0.6 17.4 %shard_map.86 = (f32[1,1024]{1,0:T(1,128)}, f32[32,1024]{1,0:T(8,128)}) custom-call(bf16[1,128,7168]{2,1,0:T(8,128)(2,1)} %hid_hbm.1, bf16[1,128,2048]{2,1,0:T(8,128)(2,1)} %grad_hbm.1, s32[1,128]{1,0:T(1,128)} %tok_hbm.1, bf16[64,7168]{1,0:T(8,128)(2,1)} %pin_hbm.1, bf16[64,2048]{1,0:T(8,128)(2,1)} %pout_hbm.1, bf16[128,4096]{1,0:T(8,128)(2,1)} %test_hbm.1, ...), custom_call_target="tpu_custom_call" | custom-call | flops 300000000 | bytes 5000000 | tf_op jit(solution)/shard_map/pallas_call | solution.py:198
  18.1 1.3 %copy.11 = f32[1,1024]{1,0:T(1,128)} copy(f32[1,1024]{1,0:T(1,128)} %get-tuple-element.4) | data formatting | bytes 8192
  19.4 1.6 %copy.12 = f32[32,1024]{1,0:T(8,128)} copy(f32[32,1024]{1,0:T(8,128)} %get-tuple-element.5) | data formatting | bytes 262144

commit v3 on v2

--- a/solution.py
+++ b/solution.py
@@ -186,7 +186,8 @@
         copy.wait_send()
 
 
-def fused(n, hidden_acts, out_grads, token_ids, proj_in, proj_out, test_feats, resample_counts):
+def fused(n, *operands):
+    hidden_acts, _, _, _, proj_out, test_feats, resample_counts = operands
     _, tokens, units = hidden_acts.shape
     rank, model = proj_out.shape
     tests = test_feats.shape[0]
@@ -221,10 +222,10 @@
             dma((2,)),
         ] + [dma((n - 1,))] * 6,
         compiler_params=pltpu.CompilerParams(
-            collective_id=0, has_side_effects=True, vmem_limit_bytes=60 * 1024 * 1024
+            collective_id=0, has_side_effects=True, vmem_limit_bytes=32 * 1024 * 1024
         ),
         cost_estimate=pl.CostEstimate(flops=300_000_000, bytes_accessed=5_000_000, transcendentals=0),
-    )(hidden_acts, out_grads, token_ids, proj_in, proj_out, test_feats, resample_counts)
+    )(*[pltpu.with_memory_space_constraint(x, pltpu.HBM) for x in operands])
 
 
 def solution(mesh):

time: 21.1 us -> 18.8 us (0.89)
  local copies, waits for them, and re-layouts: 2.85 us -> 1.25 us
  Pallas kernels: 17.4 us -> 16.8 us
    unnamed x2, local copies, waits for them, and re-layouts: 2.85 us -> 1.25 us
    pallas_call x1, Pallas kernels: 17.4 us -> 16.8 us  [fused(): pl.pallas_call(functools.partial(kernel, n, chunks), out_shape=(jax.Shape...]
where the time goes in v3:
time: 18.8 us; the launch traced here: 18.7 us
  Pallas kernels  16.8 us (89%)
  local copies, waits for them, and re-layouts  1.25 us (7%)
  between operations  0.64 us (3%)
    pallas_call x1, Pallas kernels, fused(): pl.pallas_call(functools.partial(kernel, n, chunks), out_shape=(jax.Shape...  16.8 us
    unnamed x2, local copies, waits for them, and re-layouts  1.25 us

profile of v3, /device:TPU:0, one launch (start us, length us, event | category | flops | bytes accessed | tf_op | source)
XLA Modules:
  0.0 18.7 jit_solution(8444608189716321969)
XLA Ops:
  0.6 16.8 %shard_map.86 = (f32[1,1024]{1,0:T(1,128)S(1)}, f32[32,1024]{1,0:T(8,128)S(1)}) custom-call(bf16[1,128,7168]{2,1,0:T(8,128)(2,1)} %hid_hbm.1, bf16[1,128,2048]{2,1,0:T(8,128)(2,1)} %grad_hbm.1, s32[1,128]{1,0:T(1,128)} %tok_hbm.1, bf16[64,7168]{1,0:T(8,128)(2,1)} %pin_hbm.1, bf16[64,2048]{1,0:T(8,128)(2,1)} %pout_hbm.1, bf16[128,4096]{1,0:T(8,128)(2,1)} %test_hbm.1, ...), custom_call_target="tpu_custom_call" | custom-call | flops 300000000 | bytes 5000000 | tf_op jit(solution)/shard_map/pallas_call | solution.py:199
  17.4 0.6 %copy.11 = f32[1,1024]{1,0:T(1,128)} copy(f32[1,1024]{1,0:T(1,128)S(1)} %get-tuple-element.4) | data formatting | bytes 8192
  18.0 0.7 %copy.12 = f32[32,1024]{1,0:T(8,128)} copy(f32[32,1024]{1,0:T(8,128)S(1)} %get-tuple-element.5) | data formatting | bytes 262144

commit v4 on v3

--- a/solution.py
+++ b/solution.py
@@ -49,6 +49,20 @@
     return (score_local, boot_sums)
 
 
+def partners(me, n):
+    if n & (n - 1):
+        return [lax.rem(me + k, n) for k in range(1, n)], [lax.rem(me + n - k, n) for k in range(1, n)]
+    peers = []
+    for k in range(n - 1, 0, -1):
+        peer, bit = me, 1
+        while bit < n:
+            if k & bit:
+                peer = peer + bit * (1 - 2 * lax.rem(me // bit, 2))
+            bit *= 2
+        peers.append(peer)
+    return peers, peers
+
+
 def kernel(
     n, chunks,
     hid_hbm, grad_hbm, tok_hbm, pin_hbm, pout_hbm, test_hbm, cnt_hbm,
@@ -62,13 +76,7 @@
     half = rank // 2
     tests = test.shape[0]
     boots = boot_ref.shape[0]
-    peers = [lax.rem(me + k, n) for k in range(1, n)]
-    froms = [lax.rem(me + n - k, n) for k in range(1, n)]
-
-    barrier = pltpu.get_barrier_semaphore()
-    pl.semaphore_signal(barrier, inc=1, device_id={"tensor": 1 - core}, device_id_type=MESH)
-    for peer in peers:
-        pl.semaphore_signal(barrier, inc=1, device_id={"dp": peer}, device_id_type=MESH)
+    peers, froms = partners(me, n)
 
     def load(src, dst, sem):
         copy = pltpu.make_async_copy(src, dst, sem)
@@ -88,7 +96,11 @@
     mine = pl.ds(me, 1)
     load_cnt = load(cnt_hbm, cnt.at[mine, :], load_sem.at[2])
     load_tok = load(tok_hbm, tok, load_sem.at[3])
-    load_test = load(test_hbm, test, load_sem.at[4])
+
+    barrier = pltpu.get_barrier_semaphore()
+    pl.semaphore_signal(barrier, inc=1, device_id={"tensor": 1 - core}, device_id_type=MESH)
+    for peer in peers:
+        pl.semaphore_signal(barrier, inc=1, device_id={"dp": peer}, device_id_type=MESH)
 
     load_pout.wait()
     load_grad.wait()
@@ -100,6 +112,7 @@
         cols = slice(c * width, (c + 1) * width)
         term = lax.dot_general(pin[:, cols], hid[:, cols], NT, preferred_element_type=F32)
         total = term if total is None else total + term
+    load_test = load(test_hbm, test, load_sem.at[4])
     part[rank:, :] = total
 
     pl.semaphore_wait(barrier, n)
@@ -127,7 +140,6 @@
             device_id={"dp": peers[k]}, device_id_type=MESH,
         ).wait_recv()
 
-    to_all(cnt.at[mine, :], cnt_send, cnt_recv)
     load_tok.wait()
     live = (tok[...] != 0).astype(F32)
     live_count = jnp.sum(live, axis=1, keepdims=True)
@@ -149,6 +161,25 @@
     )
     feats[me] = (grads / live_count).astype(jnp.bfloat16)
     to_all(feats.at[me], feat_send, feat_recv)
+    to_all(cnt.at[mine, :], cnt_send, cnt_recv)
+
+    def widen(source):
+        rows = pl.ds(pl.multiple_of(source * half, half), half)
+        wide[rows, :] = feats[source].astype(F32)
+
+    widen(me)
+    load_test.wait()
+    for k in range(n - 1):
+        arrived(feats.at[froms[k]], k, feat_send, feat_recv)
+        widen(froms[k])
+    flat = jnp.concatenate([wide[pl.ds(r, n, stride=half), :] for r in range(half)], axis=1)
+    scores = lax.dot_general(flat.astype(jnp.bfloat16), test[...], NT, preferred_element_type=F32)
+
+    def place(source):
+        return pl.ds(pl.multiple_of(source * tests, tests), tests)
+
+    every[:, place(me)] = scores
+    to_all(every.at[:, place(me)], sc_send, sc_recv)
 
     for k in range(n - 1):
         arrived(cnt.at[pl.ds(froms[k], 1), :], k, cnt_send, cnt_recv)
@@ -158,28 +189,13 @@
     my_counts = lax.dot_general(
         pick, cnt[...].astype(F32), NT, precision=lax.Precision.HIGHEST, preferred_element_type=F32
     )
-
-    def widen(source):
-        rows = pl.ds(pl.multiple_of(source * half, half), half)
-        wide[rows, :] = feats[source].astype(F32)
-
-    widen(me)
-    load_test.wait()
-    for k in range(n - 1):
-        arrived(feats.at[froms[k]], k, feat_send, feat_recv)
-        widen(froms[k])
-    flat = jnp.concatenate([wide[pl.ds(r, n, stride=half), :] for r in range(half)], axis=1)
-    scores = lax.dot_general(flat.astype(jnp.bfloat16), test[...], NT, preferred_element_type=F32)
-
-    def place(source):
-        return pl.ds(pl.multiple_of(source * tests, tests), tests)
-
-    every[:, place(me)] = scores
-    to_all(every.at[:, place(me)], sc_send, sc_recv)
     for k in range(n - 1):
         arrived(every.at[:, place(froms[k])], k, sc_send, sc_recv)
     score_ref[...] = every[mine, :]
-    boot_ref[...] = jnp.dot(my_counts, every[...], precision=lax.Precision.HIGHEST, preferred_element_type=F32)
+    sums = my_counts[:, 0:1] * every[0:1, :]
+    for e in range(1, n):
+        sums = sums + my_counts[:, e:e + 1] * every[e:e + 1, :]
+    boot_ref[...] = sums
 
     pair.wait_send()
     for copy in sends:
@@ -192,7 +208,7 @@
     rank, model = proj_out.shape
     tests = test_feats.shape[0]
     boots = resample_counts.shape[1]
-    chunks = 4 if units % (4 * 128) == 0 else 1
+    chunks = 2 if units % (2 * 128) == 0 else 1
     dma = pltpu.SemaphoreType.DMA
     in_hbm = pl.BlockSpec(memory_space=pl.ANY)
     vmem = pl.BlockSpec(memory_space=pltpu.VMEM)

time: 18.8 us -> 18.3 us (0.973)
  Pallas kernels: 16.8 us -> 16.2 us
    pallas_call x1, Pallas kernels: 16.8 us -> 16.2 us  [fused(): pl.pallas_call(functools.partial(kernel, n, chunks), out_shape=(jax.Shape...]
where the time goes in v4:
time: 18.3 us; the launch traced here: 18.1 us
  Pallas kernels  16.2 us (89%)
  local copies, waits for them, and re-layouts  1.25 us (7%)
  between operations  0.64 us (3%)
    pallas_call x1, Pallas kernels, fused(): pl.pallas_call(functools.partial(kernel, n, chunks), out_shape=(jax.Shape...  16.2 us
    unnamed x2, local copies, waits for them, and re-layouts  1.25 us

profile of v4, /device:TPU:0, one launch (start us, length us, event | category | flops | bytes accessed | tf_op | source)
XLA Modules:
  0.0 18.1 jit_solution(5293419041283800788)
XLA Ops:
  0.6 16.2 %shard_map.86 = (f32[1,1024]{1,0:T(1,128)S(1)}, f32[32,1024]{1,0:T(8,128)S(1)}) custom-call(bf16[1,128,7168]{2,1,0:T(8,128)(2,1)} %hid_hbm.1, bf16[1,128,2048]{2,1,0:T(8,128)(2,1)} %grad_hbm.1, s32[1,128]{1,0:T(1,128)} %tok_hbm.1, bf16[64,7168]{1,0:T(8,128)(2,1)} %pin_hbm.1, bf16[64,2048]{1,0:T(8,128)(2,1)} %pout_hbm.1, bf16[128,4096]{1,0:T(8,128)(2,1)} %test_hbm.1, ...), custom_call_target="tpu_custom_call" | custom-call | flops 300000000 | bytes 5000000 | tf_op jit(solution)/shard_map/pallas_call | solution.py:215
  16.9 0.6 %copy.11 = f32[1,1024]{1,0:T(1,128)} copy(f32[1,1024]{1,0:T(1,128)S(1)} %get-tuple-element.4) | data formatting | bytes 8192
  17.5 0.7 %copy.12 = f32[32,1024]{1,0:T(8,128)} copy(f32[32,1024]{1,0:T(8,128)S(1)} %get-tuple-element.5) | data formatting | bytes 262144

commit v5 on v4

--- a/solution.py
+++ b/solution.py
@@ -149,16 +149,14 @@
     out_even = (part[even, :] + other[even, :]) * live
     out_odd = (part[odd, :] + other[odd, :]) * live
     in_feat = part[rank:, :] + other[rank:, :]
-    blank = jnp.zeros_like(in_feat)
-    grads = lax.dot_general(
-        jnp.concatenate([out_even, out_odd], axis=1),
-        jnp.concatenate(
-            [jnp.concatenate([in_feat, blank], axis=1), jnp.concatenate([blank, in_feat], axis=1)], axis=0
-        ),
+    both = lax.dot_general(
+        jnp.concatenate([out_even, out_odd], axis=0),
+        in_feat,
         NT,
         precision=lax.Precision.HIGHEST,
         preferred_element_type=F32,
     )
+    grads = jnp.concatenate([both[:half], both[half:]], axis=1)
     feats[me] = (grads / live_count).astype(jnp.bfloat16)
     to_all(feats.at[me], feat_send, feat_recv)
     to_all(cnt.at[mine, :], cnt_send, cnt_recv)

time: 18.3 us -> 18.3 us (level)
  no operation moved by 1% of the time
where the time goes in v5:
time: 18.3 us; the launch traced here: 18.1 us
  Pallas kernels  16.2 us (89%)
  local copies, waits for them, and re-layouts  1.25 us (7%)
  between operations  0.64 us (3%)
    pallas_call x1, Pallas kernels, fused(): pl.pallas_call(functools.partial(kernel, n, chunks), out_shape=(jax.Shape...  16.2 us
    unnamed x2, local copies, waits for them, and re-layouts  1.25 us

profile of v5, /device:TPU:0, one launch (start us, length us, event | category | flops | bytes accessed | tf_op | source)
XLA Modules:
  0.0 18.1 jit_solution(3253263192081968399)
XLA Ops:
  0.6 16.2 %shard_map.86 = (f32[1,1024]{1,0:T(1,128)S(1)}, f32[32,1024]{1,0:T(8,128)S(1)}) custom-call(bf16[1,128,7168]{2,1,0:T(8,128)(2,1)} %hid_hbm.1, bf16[1,128,2048]{2,1,0:T(8,128)(2,1)} %grad_hbm.1, s32[1,128]{1,0:T(1,128)} %tok_hbm.1, bf16[64,7168]{1,0:T(8,128)(2,1)} %pin_hbm.1, bf16[64,2048]{1,0:T(8,128)(2,1)} %pout_hbm.1, bf16[128,4096]{1,0:T(8,128)(2,1)} %test_hbm.1, ...), custom_call_target="tpu_custom_call" | custom-call | flops 300000000 | bytes 5000000 | tf_op jit(solution)/shard_map/pallas_call | solution.py:213
  16.8 0.6 %copy.11 = f32[1,1024]{1,0:T(1,128)} copy(f32[1,1024]{1,0:T(1,128)S(1)} %get-tuple-element.4) | data formatting | bytes 8192
  17.4 0.7 %copy.12 = f32[32,1024]{1,0:T(8,128)} copy(f32[32,1024]{1,0:T(8,128)S(1)} %get-tuple-element.5) | data formatting | bytes 262144
